TPU v7x, 256 devices: a whole 4x4x8 slice. The times are simulated.
256 devices in a mesh: expert: 64 (over z, x, core), help: 4 (over y).
Axes of the slice: x: 4, y: 4, z: 8, core: 2. Of those that a mesh axis runs over, the one named last changes fastest.
Arguments:
- activations: bfloat16 [65536, 8, 1024], P(('expert', 'help')), may hold values from -60 to 60
- routes: int32 [65536, 8], P(('expert', 'help')), may hold values from 0 to 255, all different within a row; in each aligned block of 256 rows (0 to 255, 256 to 511, ...) at most 16 rows name the same one
- owner_map: int32 [256], replicated, may hold values from 0 to 255, each once
- damp_pct: int32 [256], P(('expert', 'help')), may hold values from 5 to 20
- scale_code: int32 [256, 3584], P(('expert', 'help')), may hold values from 8 to 32
- weight_panel: bfloat16 [256, 128, 3584], P(('expert', 'help')), may hold values from -4 to 4
Outputs:
- quantized: float32 [256, 128, 3584], P(('expert', 'help'))
- factor_strip: float32 [256, 128, 1024], P(('expert', 'help'))
Inputs may be any that keep to these rules, and one draw needn't show every extreme that they name: `routes`: each token names 8 distinct experts. Among the 256 tokens of one device no expert is named more than 16 times, and some device reaches 16. `owner_map`: each owner slot is named by exactly one expert.
All inputs are finite; a program needn't handle non-finite values.
Results may differ from a plain program's by a relative error of at most 0.0003.
Values may be sent and summed in bfloat16 or wider, within the bound.
No kernel may reach another device: no remote copies, remote signals or barrier semaphores. Data moves between devices by JAX's collectives and lax.ppermute only.
A program may use at most 128 MiB of HBM per device.

v0:
```python
import jax
import jax.numpy as jnp
from jax import lax
from jax.sharding import PartitionSpec as P

two_pi = 6.283185307179586


def soft_level(values, step):
    scaled = values / step
    smooth = scaled - jnp.sin(two_pi * scaled) / two_pi
    return step * jnp.clip(smooth, -8.0, 7.0)


def gram_items(received):
    return jnp.einsum("sncf,sncg->nfg", received, received, preferred_element_type=jnp.float32)


def quantize_blocked(panel, strip, step):
    panel_size = panel.shape[0]
    head = strip[:, :panel_size]
    positions = jnp.arange(16, dtype=jnp.int32)
    work = panel
    finished = []
    for block in range(panel_size // 16):
        begin = block * 16
        rows_now = work[begin : begin + 16]
        coeff = head[begin : begin + 16, begin : begin + 16]

        def turn(column, carry):
            current, levels, errors = carry
            values = lax.dynamic_index_in_dim(current, column, 0, keepdims=False)
            coeff_row = lax.dynamic_index_in_dim(coeff, column, 0, keepdims=False)
            pivot = lax.dynamic_index_in_dim(coeff_row, column, 0, keepdims=False)
            level = soft_level(values, step)
            error = (values - level) / pivot
            later = positions > column
            current = (
                current
                - jnp.where(later, coeff_row, jnp.zeros_like(coeff_row))[:, None] * error[None, :]
            )
            levels = lax.dynamic_update_index_in_dim(levels, level, column, 0)
            errors = lax.dynamic_update_index_in_dim(errors, error, column, 0)
            return (current, levels, errors)

        empty_block = jnp.zeros_like(rows_now)
        unused, levels, errors = lax.fori_loop(0, 16, turn, (rows_now, empty_block, empty_block))
        finished.append(levels)
        if begin + 16 < panel_size:
            after = head[begin : begin + 16, begin + 16 :]
            update = jnp.dot(
                after.T, errors, precision=lax.Precision.HIGHEST, preferred_element_type=jnp.float32
            )
            work = work.at[begin + 16 :].add(-update)
    return jnp.concatenate(finished, axis=0)


def shards(activations, routes, owner_map, damp_pct, scale_code, weight_panel):
    tok_dev, top_count, hidden_width = activations.shape
    experts = owner_map.shape[0]
    owners = lax.axis_size("expert")
    per_owner = experts // owners
    capacity = 2 * tok_dev * top_count // experts
    flat_routes = routes.reshape(-1)
    expert_ids = jnp.arange(experts, dtype=jnp.int32)
    picked = (flat_routes[:, None] == expert_ids[None, :]).astype(jnp.int32)
    slot_ids = jnp.sum(picked * owner_map[None, :], axis=1)
    by_slot = (slot_ids[:, None] == expert_ids[None, :]).astype(jnp.int32)
    running = jnp.cumsum(by_slot, axis=0)
    position = jnp.sum(running * by_slot, axis=1) - 1
    target = slot_ids * capacity + position
    outbound = jnp.zeros((experts * capacity, hidden_width), jnp.bfloat16)
    outbound = outbound.at[target].set(activations.reshape(-1, hidden_width))
    outbound = outbound.reshape(owners, per_owner, capacity, hidden_width)
    partials = gram_items(
        lax.all_to_all(outbound, "expert", split_axis=0, concat_axis=0, tiled=True)
    )
    gram_sum = lax.psum_scatter(partials, "help", scatter_dimension=0, tiled=True)
    hessian = gram_sum[0] * (2.0 / (tok_dev * top_count))
    strength = damp_pct[0].astype(jnp.float32) / 100.0
    damped = hessian + strength * jnp.mean(jnp.diagonal(hessian)) * jnp.eye(
        hidden_width, dtype=jnp.float32
    )
    lower = jnp.linalg.cholesky(damped)
    panel_size = weight_panel.shape[1]
    leading = jnp.eye(hidden_width, panel_size, dtype=jnp.float32)
    inverse_rows = jax.scipy.linalg.cho_solve((lower, True), leading).T
    head_lower = jnp.linalg.cholesky(inverse_rows[:, :panel_size])
    strip = jax.scipy.linalg.solve_triangular(head_lower, inverse_rows, lower=True)
    step = scale_code[0].astype(jnp.float32) / 32.0
    levels = quantize_blocked(weight_panel[0].astype(jnp.float32), strip, step)
    return (levels[None], strip[None])


def solution(mesh):
    in_specs = (
        P(("expert", "help"), None, None),
        P(("expert", "help"), None),
        P(),
        P(("expert", "help")),
        P(("expert", "help"), None),
        P(("expert", "help"), None, None),
    )
    out_specs = (P(("expert", "help"), None, None), P(("expert", "help"), None, None))
    return jax.shard_map(shards, mesh=mesh, in_specs=in_specs, out_specs=out_specs, check_vma=False)
```

profile of v0, /device:TPU:1, one launch (start us, length us, event | category | flops | bytes accessed | tf_op | source)
XLA Modules:
  0.0 1150.2 jit_solution(11514852127765580948)
XLA Ops:
  8.1 1.4 select_reduce_fusion
  12.5 15.3 %scatter_custom_fusion = bf16[4096,1024]{1,0:T(8,128)(2,1)} fusion(s32[2048]{0:T(1024)S(1)} %bitcast.242, bf16[256,8,1024]{2,1,0:T(8,128)(2,1)} %param.36, bf16[]{:T(256)} %constant.1650.clone.1), kind=kCustom, calls=%fused_computation.62 | custom fusion | bytes 12582914 | tf_op jit(solution)/shard_map/scatter | solution.py:73
  27.7 198.1 %all_to_all.5 = bf16[64,4,16,1024]{3,2,1,0:T(8,128)(2,1)} all-to-all(bf16[64,4,16,1024]{3,2,1,0:T(8,128)(2,1)} %bitcast.235), channel_id=1, replica_groups=mesh['expert'=64,'help'=4] {'expert'}, dimensions={0} | all-to-all | bytes 16777216 | tf_op jit(solution)/shard_map/all_to_all | solution.py:76
  225.8 17.0 %convolution_bitcast_fusion = f32[4,1024,1024]{1,2,0:T(8,128)} fusion(bf16[64,4,16,1024]{3,2,1,0:T(8,128)(2,1)} %all_to_all.5), kind=kOutput, calls=%fused_computation.44 | convolution fusion | flops 8589934592 | bytes 25165824 | tf_op jit(solution)/shard_map/sncf,sncg->nfg/dot_general | solution.py:16
  244.4 147.0 %reduce-scatter.2.cloned.1.call-done = f32[1,1024,1024]{1,2,0:T(8,128)} async-done(((f32[4,1024,1024]{1,2,0:T(8,128)}), f32[1,1024,1024]{1,2,0:T(8,128)}) %reduce-scatter.2.cloned.1.call-update) | async-done | bytes 4194320 | tf_op jit(solution)/shard_map/reduce_scatter | solution.py:78
  391.4 5.0 multiply_bitcast_fusion
  396.4 17.3 %gather_fusion = f32[1024]{0:T(1024)S(1)} fusion(f32[1024,1024]{0,1:T(8,128)} %multiply_bitcast_fusion, s32[1024]{0:T(1024)S(1)} %bitcast.234), kind=kCustom, calls=%fused_computation | custom fusion | bytes 16384 | tf_op jit(solution)/shard_map/jit(diagonal)/cond/branch_0_fun/gather | solution.py:81
  415.1 5.0 select_add_fusion
  420.1 5.5 copy.56
  425.6 4.5 fusion.23
  430.1 1.9 copy-done.2
  432.0 11.7 %cholesky.195 = f32[128,128]{1,0:T(8,128)S(1)} custom-call(f32[128,128]{1,0:T(8,128)S(1)} %cholesky.529), custom_call_target="Cholesky" | custom-call | tf_op jit(solution)/shard_map/jit(cholesky)/cholesky | solution.py:84
  443.8 9.8 custom-call.73
  453.6 1.5 fusion.39
  455.1 1.6 convolution_subtract_fusion
  457.5 11.7 %cholesky.213 = f32[128,128]{1,0:T(8,128)S(1)} custom-call(f32[128,128]{1,0:T(8,128)S(1)} %cholesky.533), custom_call_target="Cholesky" | custom-call | tf_op jit(solution)/shard_map/jit(cholesky)/cholesky | solution.py:84
  470.6 9.8 custom-call.74
  482.0 2.0 copy-done
  483.9 2.4 convolution_subtract_fusion.1
  486.3 11.7 %cholesky.240 = f32[128,128]{1,0:T(8,128)S(1)} custom-call(f32[128,128]{1,0:T(8,128)S(1)} %cholesky.538), custom_call_target="Cholesky" | custom-call | tf_op jit(solution)/shard_map/jit(cholesky)/cholesky | solution.py:84
  498.8 9.8 custom-call.75
  509.9 3.6 convolution_subtract_fusion.2
  513.5 11.7 %cholesky.429 = f32[128,128]{1,0:T(8,128)S(1)} custom-call(f32[128,128]{1,0:T(8,128)S(1)} %cholesky.543), custom_call_target="Cholesky" | custom-call | tf_op jit(solution)/shard_map/jit(cholesky)/cholesky | solution.py:84
  526.0 9.8 custom-call.76
  536.9 3.2 convolution_subtract_fusion.3
  540.1 11.8 %cholesky.448 = f32[128,128]{1,0:T(8,128)S(1)} custom-call(f32[128,128]{1,0:T(8,128)S(1)} %cholesky.548), custom_call_target="Cholesky" | custom-call | tf_op jit(solution)/shard_map/jit(cholesky)/cholesky | solution.py:84
  552.7 9.8 custom-call.77
  563.6 3.1 convolution_subtract_fusion.4
  566.8 11.7 %cholesky.468 = f32[128,128]{1,0:T(8,128)S(1)} custom-call(f32[128,128]{1,0:T(8,128)S(1)} %cholesky.553), custom_call_target="Cholesky" | custom-call | tf_op jit(solution)/shard_map/jit(cholesky)/cholesky | solution.py:84
  579.2 9.8 custom-call.78
  590.0 3.1 convolution_subtract_fusion.5
  593.1 11.7 %cholesky.488 = f32[128,128]{1,0:T(8,128)S(1)} custom-call(f32[128,128]{1,0:T(8,128)S(1)} %cholesky.558), custom_call_target="Cholesky" | custom-call | tf_op jit(solution)/shard_map/jit(cholesky)/cholesky | solution.py:84
  605.6 9.8 custom-call.79
  616.4 2.1 convolution_subtract_fusion.16
  618.5 11.7 %cholesky.506 = f32[128,128]{1,0:T(8,128)S(1)} custom-call(f32[128,128]{1,0:T(8,128)S(1)} %convolution_subtract_fusion.16), custom_call_target="Cholesky" | custom-call | tf_op jit(solution)/shard_map/jit(cholesky)/cholesky | solution.py:84
  640.5 4.8 select_select_fusion
  645.4 28.7 %while.174 = (s32[]{:T(128)}, f32[1024,1024]{0,1:T(8,128)}, s32[8,2]{0,1:T(2,128)S(1)}, f32[8,128,128]{2,1,0:T(8,128)}, s32[]{:T(128)}) while((s32[]{:T(128)}, f32[1024,1024]{0,1:T(8,128)}, s32[8,2]{0,1:T(2,128)S(1)}, f32[8,128,128]{2,1,0:T(8,128)}, s32[]{:T(128)}) %tuple.417), condition=%wide.while_cond.7, body=%wide.while_body.7.sunk | while | flops 2 | bytes 393829 | solution.py:87
  646.0 2.3 dynamic-slice.119
  649.6 2.3 dynamic-slice.119
  653.2 2.3 dynamic-slice.119
  656.8 2.3 dynamic-slice.119
  660.4 2.3 dynamic-slice.119
  664.0 2.3 dynamic-slice.119
  667.6 2.3 dynamic-slice.119
  671.2 2.2 dynamic-slice.119
  674.1 79.6 %custom-call.80 = f32[8,128,128]{1,2,0:T(8,128)S(1)} custom-call(f32[8,128,128]{2,1,0:T(8,128)} %get-tuple-element.1659), custom_call_target="InvertDiagBlocksLowerTriangular" | custom-call | tf_op jit(solution)/shard_map/jit(_cho_solve)/triangular_solve | solution.py:87
  757.1 1.4 convolution_subtract_fusion.20
  758.8 1.5 convolution_subtract_fusion.19
  760.7 1.7 convolution_subtract_fusion.13
  769.9 11.9 %cholesky.518 = f32[128,128]{1,0:T(8,128)S(1)} custom-call(f32[128,128]{1,0:T(8,128)S(1)} %fusion.99), custom_call_target="Cholesky" | custom-call | tf_op jit(solution)/shard_map/jit(cholesky)/cholesky | solution.py:88
  783.2 9.8 custom-call.81
  794.5 40.7 %while.175 = (s32[]{:T(128)}, f32[16,3584]{1,0:T(8,128)S(1)}, f32[16,3584]{1,0:T(8,128)S(1)}, f32[16,3584]{1,0:T(8,128)S(1)}, f32[16,16]{1,0:T(8,128)S(1)}, /*in...) while((s32[]{:T(128)}, f32[16,3584]{1,0:T(8,128)S(1)}, f32[16,3584]{1,0:T(8,128)S(1)}, ...), condition=%wide.region_26.27_spmd.clone, body=%wide.region_25.26_spmd.clone.sunk | while | flops 143395 | bytes 603465 | solution.py:47
  835.1 2.3 fusion.16
  838.7 42.7 %while.176 = (s32[]{:T(128)}, f32[16,3584]{1,0:T(8,128)S(1)}, f32[16,3584]{1,0:T(8,128)S(1)}, f32[16,3584]{1,0:T(8,128)S(1)}, f32[16,16]{1,0:T(8,128)S(1)}, /*in...) while((s32[]{:T(128)}, f32[16,3584]{1,0:T(8,128)S(1)}, f32[16,3584]{1,0:T(8,128)S(1)}, ...), condition=%wide.region_28.29_spmd.clone, body=%wide.region_27.28_spmd.clone.sunk | while | flops 143395 | bytes 603465 | solution.py:47
  881.3 2.7 fusion.17
  884.2 40.7 %while.177 = (s32[]{:T(128)}, f32[16,3584]{1,0:T(8,128)S(1)}, f32[16,3584]{1,0:T(8,128)S(1)}, f32[16,3584]{1,0:T(8,128)S(1)}, f32[16,16]{1,0:T(8,128)S(1)}, /*in...) while((s32[]{:T(128)}, f32[16,3584]{1,0:T(8,128)S(1)}, f32[16,3584]{1,0:T(8,128)S(1)}, ...), condition=%wide.region_30.31_spmd.clone, body=%wide.region_29.30_spmd.clone.sunk | while | flops 143395 | bytes 603465 | solution.py:47
  925.5 1.9 fusion.18
  927.5 42.6 %while.178 = (s32[]{:T(128)}, f32[16,3584]{1,0:T(8,128)S(1)}, f32[16,3584]{1,0:T(8,128)S(1)}, f32[16,3584]{1,0:T(8,128)S(1)}, f32[16,16]{1,0:T(8,128)S(1)}, /*in...) while((s32[]{:T(128)}, f32[16,3584]{1,0:T(8,128)S(1)}, f32[16,3584]{1,0:T(8,128)S(1)}, ...), condition=%wide.region_32.33_spmd.clone, body=%wide.region_31.32_spmd.clone.sunk | while | flops 143395 | bytes 603465 | solution.py:47
  970.2 1.7 fusion.19
  971.9 42.7 %while.179 = (s32[]{:T(128)}, f32[16,3584]{1,0:T(8,128)S(1)}, f32[16,3584]{1,0:T(8,128)S(1)}, f32[16,3584]{1,0:T(8,128)S(1)}, f32[16,16]{1,0:T(8,128)S(1)}, /*in...) while((s32[]{:T(128)}, f32[16,3584]{1,0:T(8,128)S(1)}, f32[16,3584]{1,0:T(8,128)S(1)}, ...), condition=%wide.region_34.35_spmd.clone, body=%wide.region_33.34_spmd.clone.sunk | while | flops 143395 | bytes 603465 | solution.py:47
  1014.6 1.5 fusion.20
  1016.2 42.9 %while.180 = (s32[]{:T(128)}, f32[16,3584]{1,0:T(8,128)S(1)}, f32[16,3584]{1,0:T(8,128)S(1)}, f32[16,3584]{1,0:T(8,128)S(1)}, f32[16,16]{1,0:T(8,128)S(1)}, /*in...) while((s32[]{:T(128)}, f32[16,3584]{1,0:T(8,128)S(1)}, f32[16,3584]{1,0:T(8,128)S(1)}, ...), condition=%wide.region_36.37_spmd.clone, body=%wide.region_35.36_spmd.clone.sunk | while | flops 143395 | bytes 603465 | solution.py:47
  1060.5 42.7 %while.181 = (s32[]{:T(128)}, f32[16,3584]{1,0:T(8,128)S(1)}, f32[16,3584]{1,0:T(8,128)S(1)}, f32[16,3584]{1,0:T(8,128)S(1)}, f32[16,16]{1,0:T(8,128)S(1)}, /*in...) while((s32[]{:T(128)}, f32[16,3584]{1,0:T(8,128)S(1)}, f32[16,3584]{1,0:T(8,128)S(1)}, ...), condition=%wide.region_38.39_spmd.clone, body=%wide.region_37.38_spmd.clone.sunk | while | flops 143395 | bytes 603465 | solution.py:47
  1104.4 37.0 %while.182 = (s32[]{:T(128)}, f32[16,3584]{1,0:T(8,128)S(1)}, f32[16,3584]{1,0:T(8,128)S(1)}, f32[16,16]{1,0:T(8,128)S(1)}, f32[3584]{0:T(1024)S(1)}, /*index=5*/s32[]{:T(128)}, s32[]{:T(128)}, s32[]{:T(128)}) while((s32[]{:T(128)}, f32[16,3584]{1,0:T(8,128)S(1)}, f32[16,3584]{1,0:T(8,128)S(1)}, f32[16,16]{1,0:T(8,128)S(1)}, ...), condition=%wide.region_40.41_spmd.clone, body=%wide.region_39.40_spmd.clone.sunk | while | flops 143395 | bytes 560445 | solution.py:47
  (966 shorter events, 379.7 us)
Async XLA Ops:
  7.2 384.3 %reduce-scatter.2.cloned.1.call-start = ((), (), s32[]{:S(2)}) async-start(), calls=%async_computation.2 | async-start | bytes 20971520 | tf_op jit(solution)/shard_map/reduce_scatter | solution.py:78
  242.8 1.2 copy-start.9
  242.8 1.4 copy-start.12
  430.1 1.9 copy-start.2
  456.7 0.8 copy-start.5
  470.5 10.5 copy-start.4
  480.4 1.0 copy-start.6
  481.9 2.0 copy-start
  753.7 9.0 copy-start.1
  793.6 0.8 copy-start.10
  837.4 1.2 copy-start.3
  924.8 0.7 copy-start.7
  1060.5 81.0 %copy-start.8 = (f32[16,3584]{1,0:T(8,128)S(1)}, f32[16,3584]{1,0:T(8,128)}, u32[]{:S(2)}) copy-start(f32[16,3584]{1,0:T(8,128)} %copy-done.7) | copy-start | bytes 688132
  1141.6 1.2 copy-start.11
Sparse Core Ops, SparseCore 0:
  243.0 148.4 reduce-scatter.1
where the time goes:
time: 1160 us; the launch traced here: 1150 us
  other arithmetic  453 us (39%)
  local copies, waits for them, and re-layouts  252 us (22%)
  blocking collectives  198 us (17%)
  waiting for transfers between devices  147 us (13%)
  matrix products  72.2 us (6%)
  between operations  22.1 us (2%)
    all_to_all x1, blocking collectives, shards(): lax.all_to_all(outbound, 'expert', split_axis=0, concat_axis=0, tiled=True)  198 us
    another operation x30, other arithmetic, shards(): lower = jnp.linalg.cholesky(damped)  167 us
    reduce_scatter x1, waiting for transfers between devices, shards(): lax.psum_scatter(partials, 'help', scatter_dimension=0, tiled=True)  147 us
    div x128, other arithmetic, turn(): error = (values - level) / pivot  145 us
    another operation x3, other arithmetic, shards(): inverse_rows = jax.scipy.linalg.cho_solve((lower, True), leading).T  84.4 us
    dynamic_slice x128, local copies, waits for them, and re-layouts, turn(): pivot = lax.dynamic_index_in_dim(coeff_row, column, 0, keepdims=False)  83 us
    dynamic_update_slice x128, local copies, waits for them, and re-layouts, turn(): levels = lax.dynamic_update_index_in_dim(levels, level, column, 0)  44.3 us
    dynamic_update_slice x112, local copies, waits for them, and re-layouts, turn(): errors = lax.dynamic_update_index_in_dim(errors, error, column, 0)  38.8 us
  transfers between devices with their start and end apart: 1, of which 1 were waited for; matrix products, arithmetic and copies ran while one was open for 0% of the time, Pallas kernels for 0%

commit v1 on v0

v1 whole, which is shorter than its diff:
```python
import functools

import jax
import jax.numpy as jnp
import numpy as np
from jax import lax
from jax.experimental import pallas as pl
from jax.experimental.pallas import tpu as pltpu
from jax.sharding import PartitionSpec as P

HIGH = lax.Precision.HIGHEST
BLK = 128
GROUP = 32

def _mm(a, b):
    return jnp.dot(a, b, precision=HIGH, preferred_element_type=jnp.float32)


def _lane(v, c):
    return jnp.broadcast_to(v[:, c : c + 1], v.shape[:1] + (BLK,))


def _row(v, s):
    return jnp.broadcast_to(v[s : s + 1, :], (8, v.shape[1]))


def _sweep8(panel, first):
    cols = [_lane(panel, first + j) for j in range(8)]
    a = {(i, j): _row(cols[j], i) for j in range(8) for i in range(j + 1)}
    at = lambda i, j: a[(i, j) if i <= j else (j, i)]
    unit, pivots = {}, {}
    for k in range(7, -1, -1):
        pivots[k] = at(k, k)
        for t in range(k + 1, 8):
            unit[(k, t)] = -at(k, t)
        d = 1.0 / at(k, k)
        b = {i: at(i, k) for i in range(8) if i != k}
        u = {i: b[i] * d for i in b}
        for j in b:
            for i in b:
                if i <= j:
                    a[(i, j)] = a[(i, j)] - u[i] * b[j]
        for i in b:
            a[(i, k) if i <= k else (k, i)] = u[i]
        a[(k, k)] = -d
    sub = lax.broadcasted_iota(jnp.int32, (8, BLK), 0)
    inverse = []
    for s in range(8):
        col = -at(0, s)
        for i in range(1, 8):
            col = jnp.where(sub == i, -at(i, s), col)
        inverse.append(col)
    return inverse, unit, pivots


def negative_inverse(tiles):
    tiles = list(tiles)
    lane = lax.broadcasted_iota(jnp.int32, (8, BLK), 1)
    sub = lax.broadcasted_iota(jnp.int32, (8, BLK), 0)
    for g in range(15, -1, -1):
        first = 8 * g
        inside = (lane >= first) & (lane < first + 8)
        cols, _, _ = _sweep8(tiles[g], first)
        panel = jnp.where(inside, jnp.where(lane - first == sub, -1.0, 0.0), tiles[g])
        solved = sum(cols[s] * _row(panel, s) for s in range(8))
        rows = [_row(solved, s) for s in range(8)]
        for i in range(16):
            if i != g:
                kept = jnp.where(inside, 0.0, tiles[i])
                for s in range(8):
                    kept = kept - _lane(tiles[i], first + s) * rows[s]
                tiles[i] = kept
        tiles[g] = solved
    return tiles


def upper_inverse(tiles):
    tiles = list(tiles)
    lane = lax.broadcasted_iota(jnp.int32, (8, BLK), 1)
    sub = lax.broadcasted_iota(jnp.int32, (8, BLK), 0)
    extra = [jnp.where(lane - 8 * i == sub, 1.0, 0.0) for i in range(16)]
    out = [None] * 16
    for g in range(15, -1, -1):
        first = 8 * g
        cols, unit, pivots = _sweep8(tiles[g], first)
        own = None
        for t in range(8):
            col = jnp.where(sub == t, 1.0, 0.0)
            for s in range(t):
                col = jnp.where(sub == s, unit[(s, t)], col)
            term = col * _row(extra[g], t)
            own = term if own is None else own + term
        scale = lax.rsqrt(pivots[0])
        for s in range(1, 8):
            scale = jnp.where(sub == s, lax.rsqrt(pivots[s]), scale)
        out[g] = own * scale
        solved = sum(cols[s] * _row(tiles[g], s) for s in range(8))
        solved_extra = sum(cols[s] * _row(extra[g], s) for s in range(8))
        rows = [_row(solved, s) for s in range(8)]
        rows_extra = [_row(solved_extra, s) for s in range(8)]
        for i in range(g):
            kept, kept_extra = tiles[i], extra[i]
            for s in range(8):
                c = _lane(tiles[i], first + s)
                kept = kept - c * rows[s]
                kept_extra = kept_extra - c * rows_extra[s]
            tiles[i], extra[i] = kept, kept_extra
    return out


def strip_kernel(damp_ref, gram_ref, strip_ref, coeff_ref, coeff_t_ref, h_ref, inv_ref, *, rows_of):
    width = gram_ref.shape[0]
    blocks = width // BLK
    scale = 2.0 / rows_of
    r = lax.broadcasted_iota(jnp.int32, (BLK, BLK), 0)
    c = lax.broadcasted_iota(jnp.int32, (BLK, BLK), 1)
    diagonal = r == c
    total = jnp.zeros((8, BLK), jnp.float32)
    for k in range(blocks):
        d = jnp.where(diagonal, gram_ref[k * BLK : (k + 1) * BLK, k * BLK : (k + 1) * BLK] * scale, 0.0)
        for i in range(16):
            total = total + d[8 * i : 8 * i + 8]
    strength = damp_ref[0].astype(jnp.float32) / 100.0
    shift = strength * (jnp.sum(total) / width)
    h_ref[...] = gram_ref[...] * scale
    for k in range(blocks):
        at = slice(k * BLK, (k + 1) * BLK)
        h_ref[at, at] = h_ref[at, at] + jnp.where(diagonal, shift, 0.0)

    def eliminate(step, carry):
        k = blocks - 1 - step
        at = pl.multiple_of(k * BLK, BLK)
        mine = pl.ds(at, BLK)
        tiles = negative_inverse([h_ref[pl.ds(at + 8 * i, 8), mine] for i in range(16)])
        for i in range(16):
            inv_ref[8 * i : 8 * i + 8, :] = tiles[i]
        neg = inv_ref[...]
        panel = -_mm(neg, h_ref[mine, :])
        h_ref[mine, :] = panel
        h_ref[mine, mine] = neg
        solved = h_ref[mine, :]

        def above(i, unused):
            rows = pl.ds(pl.multiple_of(i * BLK, BLK), BLK)
            col = h_ref[rows, mine]
            h_ref[rows, mine] = jnp.zeros((BLK, BLK), jnp.float32)
            h_ref[rows, :] = h_ref[rows, :] - _mm(col, h_ref[mine, :])
            return unused

        lax.fori_loop(0, k, above, 0)
        return carry

    lax.fori_loop(0, blocks - 1, eliminate, 0)
    tiles = upper_inverse([h_ref[8 * i : 8 * i + 8, :BLK] for i in range(16)])
    for i in range(16):
        inv_ref[8 * i : 8 * i + 8, :] = tiles[i]
    strip_ref[:, :BLK] = inv_ref[...]
    strip_ref[:, BLK:] = -_mm(inv_ref[...], h_ref[:BLK, BLK:])
    head = inv_ref[...]
    coeff = head / jnp.sum(jnp.where(diagonal, head, 0.0), axis=1, keepdims=True)
    coeff_ref[...] = coeff
    coeff_t_ref[...] = coeff.T


def factor_strip(gram, damp_pct, rows_of):
    width = gram.shape[0]
    return pl.pallas_call(
        functools.partial(strip_kernel, rows_of=rows_of),
        out_shape=[
            jax.ShapeDtypeStruct((BLK, width), jnp.float32),
            jax.ShapeDtypeStruct((BLK, BLK), jnp.float32),
            jax.ShapeDtypeStruct((BLK, BLK), jnp.float32),
        ],
        in_specs=[pl.BlockSpec(memory_space=pltpu.SMEM), pl.BlockSpec(memory_space=pltpu.VMEM)],
        out_specs=[pl.BlockSpec(memory_space=pltpu.VMEM)] * 3,
        scratch_shapes=[pltpu.VMEM((width, width), jnp.float32), pltpu.VMEM((BLK, BLK), jnp.float32)],
        compiler_params=pltpu.CompilerParams(vmem_limit_bytes=40 * 1024 * 1024),
        name="factor_strip",
    )(damp_pct, gram)


def sine_coefficients(degree):
    nodes = np.cos((np.arange(400) + 0.5) * np.pi / 400) * 0.125 + 0.125
    r = np.sqrt(nodes)
    q = np.sin(2 * np.pi * r) / (2 * np.pi) / (r * (1 - 4 * nodes))
    return [float(v) for v in np.polynomial.chebyshev.Chebyshev.fit(nodes, q, degree, domain=[0, 0.25]).convert(kind=np.polynomial.Polynomial).coef]


COEF = sine_coefficients(6)


def _poly(z):
    z2 = z * z
    z4 = z2 * z2
    a = COEF[0] + COEF[1] * z
    b = COEF[2] + COEF[3] * z
    c = COEF[4] + COEF[5] * z
    return (a + b * z2) + (c + COEF[6] * z2) * z4


def level_of(values, step, per_step):
    scaled = values * per_step
    r = scaled - jnp.round(scaled)
    z = r * r
    smooth = scaled - (r * (1.0 - 4.0 * z)) * _poly(z)
    return step * jnp.clip(smooth, -8.0, 7.0)


def quantize_kernel(coeff_ref, coeff_t_ref, panel_ref, code_ref, out_ref, work_ref, lay_ref, err_ref, nat_ref):
    size, width = panel_ref.shape
    tiles = width // BLK
    pad = lay_ref.shape[0] // GROUP
    work_ref[...] = panel_ref[...].astype(jnp.float32)
    step = code_ref[...].astype(jnp.float32) / 32.0
    per_step = 1.0 / step
    for group in range(size // GROUP):
        base = group * GROUP
        for sub in range(GROUP // 8):
            for c in range(tiles):
                lay_ref[pl.ds(sub * 8 * pad + c, 8, stride=pad), :] = work_ref[base + 8 * sub : base + 8 * sub + 8, c * BLK : (c + 1) * BLK]
        for sub in range(GROUP // 8):
            now = [lay_ref[(sub * 8 + r) * pad : (sub * 8 + r) * pad + tiles, :] for r in range(8)]
            for i in range(sub * 8):
                error = err_ref[i * pad : i * pad + tiles, :]
                for r in range(8):
                    now[r] = now[r] - coeff_ref[base + i, base + sub * 8 + r] * error
            for r in range(8):
                row = sub * 8 + r
                level = level_of(now[r], step, per_step)
                error = now[r] - level
                for later in range(r + 1, 8):
                    now[later] = now[later] - coeff_ref[base + row, base + sub * 8 + later] * error
                err_ref[row * pad : row * pad + tiles, :] = error
                lay_ref[row * pad : row * pad + tiles, :] = level
        for sub in range(GROUP // 8):
            for c in range(tiles):
                out_ref[base + 8 * sub : base + 8 * sub + 8, c * BLK : (c + 1) * BLK] = lay_ref[pl.ds(sub * 8 * pad + c, 8, stride=pad), :]
        after = base + GROUP
        if after < size:
            for sub in range(GROUP // 8):
                for c in range(tiles):
                    nat_ref[8 * sub : 8 * sub + 8, c * BLK : (c + 1) * BLK] = err_ref[pl.ds(sub * 8 * pad + c, 8, stride=pad), :]
            lhs = coeff_t_ref[after:, base : base + GROUP]

            def chunk(j, unused):
                at = pl.ds(pl.multiple_of(j * 512, 512), 512)
                work_ref[after:, at] = work_ref[after:, at] - _mm(lhs, nat_ref[:, at])
                return unused

            lax.fori_loop(0, width // 512, chunk, 0)


def quantize(coeff, coeff_t, panel, code):
    size, width = panel.shape
    tiles = width // BLK
    pad = 32
    vm = pl.BlockSpec(memory_space=pltpu.VMEM)
    return pl.pallas_call(
        quantize_kernel,
        out_shape=jax.ShapeDtypeStruct((size, width), jnp.float32),
        in_specs=[pl.BlockSpec(memory_space=pltpu.SMEM), vm, vm, vm],
        out_specs=vm,
        scratch_shapes=[
            pltpu.VMEM((size, width), jnp.float32),
            pltpu.VMEM((GROUP * pad, BLK), jnp.float32),
            pltpu.VMEM((GROUP * pad, BLK), jnp.float32),
            pltpu.VMEM((GROUP, width), jnp.float32),
        ],
        compiler_params=pltpu.CompilerParams(vmem_limit_bytes=40 * 1024 * 1024),
        name="quantize",
    )(coeff, coeff_t, panel, code.reshape(tiles, BLK))


def dispatch(activations, routes, owner_map):
    tok_dev, top_count, hidden_width = activations.shape
    experts = owner_map.shape[0]
    capacity = 2 * tok_dev * top_count // experts
    flat_routes = routes.reshape(-1)
    expert_ids = jnp.arange(experts, dtype=jnp.int32)
    picked = (flat_routes[:, None] == expert_ids[None, :]).astype(jnp.int32)
    slot_ids = jnp.sum(picked * owner_map[None, :], axis=1)
    by_slot = (slot_ids[:, None] == expert_ids[None, :]).astype(jnp.int32)
    running = jnp.cumsum(by_slot, axis=0)
    position = jnp.sum(running * by_slot, axis=1) - 1
    target = slot_ids * capacity + position
    outbound = jnp.zeros((experts * capacity, hidden_width), jnp.bfloat16)
    outbound = outbound.at[target].set(activations.reshape(-1, hidden_width))
    return outbound.reshape(experts, capacity, hidden_width)


def shards(activations, routes, owner_map, damp_pct, scale_code, weight_panel):
    tok_dev, top_count, hidden_width = activations.shape
    outbound = dispatch(activations, routes, owner_map)
    received = lax.all_to_all(outbound, ("expert", "help"), split_axis=0, concat_axis=0, tiled=True)
    rows = received.reshape(-1, hidden_width)
    gram = lax.dot_general(rows, rows, (((0,), (0,)), ((), ())), preferred_element_type=jnp.float32)
    strip, coeff, coeff_t = factor_strip(gram, damp_pct, tok_dev * top_count)
    levels = quantize(coeff, coeff_t, weight_panel[0], scale_code[0])
    return (levels[None], strip[None])


def solution(mesh):
    in_specs = (
        P(("expert", "help"), None, None),
        P(("expert", "help"), None),
        P(),
        P(("expert", "help")),
        P(("expert", "help"), None),
        P(("expert", "help"), None, None),
    )
    out_specs = (P(("expert", "help"), None, None), P(("expert", "help"), None, None))
    return jax.shard_map(shards, mesh=mesh, in_specs=in_specs, out_specs=out_specs, check_vma=False)
```

time: 1160 us -> 320 us (0.28)
  other arithmetic: 453 us -> 2.98 us
  local copies, waits for them, and re-layouts: 252 us -> 17.5 us
  blocking collectives: 198 us -> 0 us
  Pallas kernels: 0 us -> 80.6 us
  matrix products: 72.2 us -> 14.7 us
  waiting for transfers between devices: 147 us -> 186 us
  between operations: 22.1 us -> 1.4 us
  starting transfers between devices: 0.04 us -> 16.7 us
    another operation x41 -> x3, other arithmetic: 275 us -> 0.6 us  [the longest x30 167 us: shards(): lower = jnp.linalg.cholesky(damped)]
    all_to_all x1 -> x0, blocking collectives: 198 us -> none  [shards(): lax.all_to_all(outbound, 'expert', split_axis=0, concat_axis=0, tiled=True)]
    all_to_all x0 -> x1, waiting for transfers between devices: none -> 186 us  [shards(): lax.all_to_all(outbound, ('expert', 'help'), split_axis=0, concat_axis=0,...]
    div x131 -> x0, other arithmetic: 149 us -> none  [the longest x128 145 us: turn(): error = (values - level) / pivot]
    reduce_scatter x1 -> x0, waiting for transfers between devices: 147 us -> none  [shards(): lax.psum_scatter(partials, 'help', scatter_dimension=0, tiled=True)]
    dynamic_update_slice x240 -> x0, local copies, waits for them, and re-layouts: 83.1 us -> none  [the longest x128 44.3 us: turn(): levels = lax.dynamic_update_index_in_dim(levels, level, column, 0)]
    dynamic_slice x128 -> x0, local copies, waits for them, and re-layouts: 83 us -> none  [turn(): pivot = lax.dynamic_index_in_dim(coeff_row, column, 0, keepdims=False)]
    pallas_call x0 -> x2, Pallas kernels: none -> 80.6 us  [the longest x1 64.1 us: factor_strip(): pl.pallas_call(functools.partial(strip_kernel, rows_of=rows_of), out_shap...]
where the time goes in v1:
time: 320 us
  waiting for transfers between devices  186 us (58%)
  Pallas kernels  80.6 us (25%)
  local copies, waits for them, and re-layouts  17.5 us (5%)
  starting transfers between devices  16.7 us (5%)
  matrix products  14.7 us (5%)
    all_to_all x1, waiting for transfers between devices, shards(): lax.all_to_all(outbound, ('expert', 'help'), split_axis=0, concat_axis=0,...  186 us
    pallas_call x1, Pallas kernels, factor_strip(): pl.pallas_call(functools.partial(strip_kernel, rows_of=rows_of), out_shap...  64.1 us
    all_to_all x1, starting transfers between devices, shards(): lax.all_to_all(outbound, ('expert', 'help'), split_axis=0, concat_axis=0,...  16.7 us
    pallas_call x1, Pallas kernels, quantize(): pl.pallas_call(quantize_kernel, out_shape=jax.ShapeDtypeStruct((size, wid...  16.5 us
    scatter x1, local copies, waits for them, and re-layouts, dispatch(): outbound = outbound.at[target].set(activations.reshape(-1, hidden_width))  15.2 us
    dot_general x1, matrix products, shards(): lax.dot_general(rows, rows, (((0,), (0,)), ((), ())), preferred_element_t...  14.7 us
  transfers between devices with their start and end apart: 1, of which 1 were waited for; matrix products, arithmetic and copies ran while one was open for 0% of the time, Pallas kernels for 0%

profile of v1, /device:TPU:1, one launch (start us, length us, event | category | flops | bytes accessed | tf_op | source)
XLA Modules:
  0.0 320.1 jit_solution(1479563276295190946)
XLA Ops:
  0.6 0.8 copy.14
  1.5 0.1 eq.38
  1.6 1.4 select_reduce_fusion
  3.0 0.1 copy.15
  3.1 0.3 fusion.4
  3.5 0.2 broadcast_add_fusion
  3.7 1.2 copy.16
  5.0 0.9 fusion.3
  5.9 15.2 %scatter_custom_fusion = bf16[4096,1024]{1,0:T(8,128)(2,1)} fusion(s32[2048]{0:T(1024)S(1)} %bitcast.29, bf16[256,8,1024]{2,1,0:T(8,128)(2,1)} %param.6, bf16[]{:T(256)} %constant.5.clone.1), kind=kCustom, calls=%fused_computation.1 | custom fusion | bytes 12582914 | tf_op jit(solution)/shard_map/scatter | solution.py:287
  21.1 0.0 copy-start.1
  21.1 16.7 %all-to-all-start = ((bf16[256,16,1024]{2,1,0:T(8,128)(2,1)}), bf16[256,16,1024]{2,1,0:T(8,128)(2,1)}, u32[]{:S(2)}, u32[]{:S(2)}) async-start(bf16[256,16,1024]{2,1,0:T(8,128)(2,1)} %bitcast.25), calls=%async_computation | async-start | bytes 16777216 | tf_op jit(solution)/shard_map/all_to_all | solution.py:294
  38.5 0.0 copy-done.1
  38.5 186.2 %all-to-all-done = bf16[256,16,1024]{2,1,0:T(8,128)(2,1)} async-done(((bf16[256,16,1024]{2,1,0:T(8,128)(2,1)}), bf16[256,16,1024]{2,1,0:T(8,128)(2,1)}, u32[]{:S(2)}, u32[]{:S(2)}) %all-to-all-start) | async-done | bytes 8388640 | tf_op jit(solution)/shard_map/all_to_all | solution.py:294
  224.8 14.7 %convolution_bitcast_fusion.gram_ref = f32[1024,1024]{1,0:T(8,128)S(1)} fusion(bf16[256,16,1024]{2,1,0:T(8,128)(2,1)} %all-to-all-done), kind=kOutput, calls=%fused_computation.4 | convolution fusion | flops 8589934592 | bytes 12582912 | tf_op jit(solution)/shard_map/dot_general | solution.py:296
  239.4 0.0 copy-start
  239.5 64.1 %factor_strip.1 = (f32[128,1024]{1,0:T(8,128)}, f32[128,128]{1,0:T(8,128)S(1)}, f32[128,128]{1,0:T(8,128)S(1)}) custom-call(s32[1]{0:T(128)S(6)} %copy.21.damp_ref, f32[1024,1024]{1,0:T(8,128)S(1)} %convolution_bitcast_fusion.gram_ref), custom_call_target="tpu_custom_call" | custom-call | tf_op jit(solution)/shard_map/factor_strip/pallas_call | solution.py:167
  303.6 0.0 copy-done
  303.6 16.5 %quantize.1 = f32[128,3584]{1,0:T(8,128)} custom-call(f32[128,128]{1,0:T(8,128)S(1)} %get-tuple-element.5.coeff_ref, f32[128,128]{1,0:T(8,128)S(1)} %get-tuple-element.6.coeff_t_ref, bf16[128,3584]{1,0:T(8,128)(2,1)S(1)} %bitcast.23, s32[28,128]{1,0:T(8,128)S(1)} %bitcast.24), custom_call_target="tpu_custom_call" | custom-call | tf_op jit(solution)/shard_map/quantize/pallas_call | solution.py:258
  (6 shorter events, 0.1 us)
Async XLA Ops:
  21.1 17.3 %copy-start.1 = (s32[1,3584]{1,0:T(1,128)S(1)}, s32[1,3584]{1,0:T(1,128)}, u32[]{:S(2)}) copy-start(s32[1,3584]{1,0:T(1,128)} %param.10) | copy-start | bytes 43012
  21.1 203.6 %all-to-all-start = ((bf16[256,16,1024]{2,1,0:T(8,128)(2,1)}), bf16[256,16,1024]{2,1,0:T(8,128)(2,1)}, u32[]{:S(2)}, u32[]{:S(2)}) async-start(bf16[256,16,1024]{2,1,0:T(8,128)(2,1)} %bitcast.25), calls=%async_computation | async-start | bytes 16777216 | tf_op jit(solution)/shard_map/all_to_all | solution.py:294
  239.4 64.1 %copy-start = (bf16[1,128,3584]{2,1,0:T(8,128)(2,1)S(1)}, bf16[1,128,3584]{2,1,0:T(8,128)(2,1)}, u32[]{:S(2)}) copy-start(bf16[1,128,3584]{2,1,0:T(8,128)(2,1)} %param.11) | copy-start | bytes 2752516
